TPU v7x, 32 devices: a whole 2x2x4 slice. The times are simulated.
32 devices in a mesh: row: 16 (over z, y, core), col: 2 (over x).
Axes of the slice: x: 2, y: 2, z: 4, core: 2. Of those that a mesh axis runs over, the one named last changes fastest.
Arguments:
- kernel: float32 [4096, 4096], P('row', 'col')
- targets: float32 [4096, 64], P('row'), may hold values from -60 to 60
Outputs:
- schur: float32 [4096, 4096], P('row', 'col')
- factor: float32 [4096, 512], P('row')
- solved: float32 [4096, 64], P('row')
All inputs are finite; a program needn't handle non-finite values.
Results may differ from a plain program's by a relative error of at most 0.00022.
Values sent between devices are 32-bit elements; how exact they have to be, the bound alone decides.
A program may use at most 64 MiB of HBM per device.

v0:
```python
import jax
import jax.numpy as jnp
from jax import lax
from jax.sharding import PartitionSpec as P

PANELS = 2


def broadcast(value, axis, source):
    kept = jnp.where(lax.axis_index(axis) == source, value, 0).astype(value.dtype)
    return lax.psum(kept, axis)


def shards(kernel, targets):
    matrix = kernel
    rhs_now = targets
    block = matrix.shape[0]
    local_blocks = matrix.shape[1] // block
    grid_cols = lax.axis_size("col")
    my_row = lax.axis_index("row")
    my_col = lax.axis_index("col")
    columns_out = []
    for step in range(PANELS):
        local = step // grid_cols
        piece = matrix[:, local * block : (local + 1) * block]
        column = broadcast(piece, "col", step % grid_cols)
        diagonal, rhs_top = (broadcast(column, "row", step), broadcast(rhs_now, "row", step))
        lower = jnp.linalg.cholesky(diagonal)
        panel = lax.linalg.triangular_solve(
            lower, column, left_side=False, lower=True, transpose_a=True
        )
        panel = jnp.where(my_row > step, panel, jnp.float32(0.0))
        top = lax.linalg.triangular_solve(lower, rhs_top, left_side=True, lower=True)
        rhs_now = jnp.where(
            my_row == step, top, rhs_now - jnp.dot(panel, top, precision=lax.Precision.HIGHEST)
        )
        columns_out.append(jnp.where(my_row == step, lower, panel))
        width = block // grid_cols
        sliced = lax.dynamic_slice_in_dim(panel, my_col * width, width, 1)
        every = lax.all_gather(sliced, "row", axis=0, tiled=True)
        every = every.reshape(local_blocks, grid_cols, block, width)
        mine = lax.all_to_all(every, "col", split_axis=1, concat_axis=3, tiled=True)
        partner = mine.reshape(local_blocks * block, block)
        matrix = matrix - jnp.dot(panel, partner.T, precision=lax.Precision.HIGHEST)
    return (matrix, jnp.concatenate(columns_out, axis=1), rhs_now)


def solution(mesh):
    return jax.shard_map(
        shards,
        mesh=mesh,
        in_specs=(P("row", "col"), P("row", None)),
        out_specs=(P("row", "col"), P("row", None), P("row", None)),
        check_vma=False,
    )
```

profile of v0, /device:TPU:5, one launch (start us, length us, event | category | flops | bytes accessed | tf_op | source)
XLA Modules:
  0.0 552.4 jit_solution(5349530323043499712)
XLA Ops:
  7.2 2.0 copy.27
  9.2 0.8 slice_select_fusion.1
  10.1 0.6 broadcast_select_fusion.3
  10.7 24.1 %all-reduce.8.cloned.1.call-done = f32[256,256]{0,1:T(8,128)} async-done(((f32[256,256]{0,1:T(8,128)}), f32[256,256]{0,1:T(8,128)}) %all-reduce.8.cloned.1.call-update) | async-done | bytes 262160 | tf_op jit(solution)/shard_map/psum | solution.py:11
  34.8 0.7 broadcast_select_fusion.1
  35.6 92.4 %all-reduce.14.cloned.1.call-done = (f32[256,256]{0,1:T(8,128)}, f32[256,64]{0,1:T(8,128)}) async-done(((f32[256,256]{0,1:T(8,128)}, f32[256,64]{0,1:T(8,128)}), (f32[256,256]{0,1:T(8,128)}, f32[256,64]{0,1:T(8,128)})) %all-reduce.14.cloned.1.call-update) | async-done | bytes 327696 | tf_op jit(solution)/shard_map/psum | solution.py:11
  128.0 1.1 copy.22
  129.1 1.0 fusion.3
  130.1 11.7 %cholesky.130 = f32[128,128]{1,0:T(8,128)S(1)} custom-call(f32[128,128]{1,0:T(8,128)S(1)} %cholesky.194), custom_call_target="Cholesky" | custom-call | tf_op jit(solution)/shard_map/jit(cholesky)/cholesky | solution.py:28
  142.0 9.8 %custom-call.17 = f32[1,128,128]{1,2,0:T(8,128)S(1)} custom-call(f32[1,128,128]{2,1,0:T(8,128)S(1)} %get-tuple-element.107), custom_call_target="InvertDiagBlocksLowerTriangular" | custom-call | tf_op jit(solution)/shard_map/jit(cholesky)/cholesky | solution.py:28
  152.4 11.7 %cholesky.147 = f32[128,128]{1,0:T(8,128)S(1)} custom-call(f32[128,128]{1,0:T(8,128)S(1)} %convolution_subtract_fusion.5), custom_call_target="Cholesky" | custom-call | tf_op jit(solution)/shard_map/jit(cholesky)/cholesky | solution.py:28
  164.3 0.6 compare_reduce_fusion.2
  166.3 4.4 while.8
  166.5 0.6 fusion.61
  167.1 1.4 dynamic-slice.17
  168.7 0.6 fusion.61
  169.2 1.4 dynamic-slice.17
  170.8 19.7 %custom-call.18 = f32[2,128,128]{1,2,0:T(8,128)S(1)} custom-call(f32[2,128,128]{2,1,0:T(8,128)S(1)} %get-tuple-element.34), custom_call_target="InvertDiagBlocksLowerTriangular" | custom-call | tf_op jit(solution)/shard_map/triangular_solve/custom-call.0 | solution.py:29
  190.8 0.3 convolution_subtract_fusion.3
  191.1 0.3 fusion.27
  191.4 0.8 fusion.7
  192.2 0.7 constant_dynamic-slice_fusion.3
  192.9 42.9 %all-gather.3.cloned.1.call-done = f32[4096,128]{0,1:T(8,128)} async-done(((f32[256,128]{0,1:T(8,128)}), f32[4096,128]{0,1:T(8,128)}) %all-gather.3.cloned.1.call-update) | async-done | bytes 2097168 | tf_op jit(solution)/shard_map/all_gather | solution.py:40
  235.8 3.0 reshape.43
  238.8 1.5 copy.26
  240.3 3.9 all-to-all-start
  244.7 24.3 %all-to-all-done = f32[8,2,256,128]{2,0,3,1:T(8,128)S(1)} async-done(((f32[8,2,256,128]{2,0,3,1:T(8,128)}), f32[8,2,256,128]{2,0,3,1:T(8,128)S(1)}, u32[]{:S(2)}, u32[]{:S(2)}) %all-to-all-start) | async-done | bytes 2097184 | tf_op jit(solution)/shard_map/all_to_all | solution.py:42
  268.9 0.9 copy.43
  269.8 0.7 copy-done.1
  270.5 3.7 convolution_subtract_fusion.1
  274.2 0.7 slice_select_fusion
  275.2 0.9 broadcast_select_fusion.2
  276.1 20.4 %all-reduce.10.cloned.1.call-done = f32[256,256]{0,1:T(8,128)} async-done(((f32[256,256]{0,1:T(8,128)}), f32[256,256]{0,1:T(8,128)}) %all-reduce.10.cloned.1.call-update) | async-done | bytes 262160 | tf_op jit(solution)/shard_map/psum | solution.py:11
  296.5 0.7 broadcast_select_fusion
  297.5 92.1 %all-reduce.12.cloned.1.call-done = (f32[256,256]{0,1:T(8,128)}, f32[256,64]{0,1:T(8,128)}) async-done(((f32[256,256]{0,1:T(8,128)}, f32[256,64]{0,1:T(8,128)}), (f32[256,256]{0,1:T(8,128)}, f32[256,64]{0,1:T(8,128)})) %all-reduce.12.cloned.1.call-update) | async-done | bytes 327696 | tf_op jit(solution)/shard_map/psum | solution.py:11
  389.6 1.1 copy.29
  390.7 1.0 fusion.2
  391.7 11.7 %cholesky.164 = f32[128,128]{1,0:T(8,128)S(1)} custom-call(f32[128,128]{1,0:T(8,128)S(1)} %cholesky.197), custom_call_target="Cholesky" | custom-call | tf_op jit(solution)/shard_map/jit(cholesky)/cholesky | solution.py:28
  403.6 9.8 %custom-call.19 = f32[1,128,128]{1,2,0:T(8,128)S(1)} custom-call(f32[1,128,128]{2,1,0:T(8,128)S(1)} %get-tuple-element.105), custom_call_target="InvertDiagBlocksLowerTriangular" | custom-call | tf_op jit(solution)/shard_map/jit(cholesky)/cholesky | solution.py:28
  414.0 11.7 %cholesky.181 = f32[128,128]{1,0:T(8,128)S(1)} custom-call(f32[128,128]{1,0:T(8,128)S(1)} %convolution_subtract_fusion.4), custom_call_target="Cholesky" | custom-call | tf_op jit(solution)/shard_map/jit(cholesky)/cholesky | solution.py:28
  425.8 0.6 compare_reduce_fusion.1
  426.5 0.6 compare_reduce_fusion
  428.5 4.5 while.9
  428.8 0.6 fusion.62
  429.3 1.4 dynamic-slice.19
  430.9 0.6 fusion.62
  431.5 1.4 dynamic-slice.19
  433.0 19.7 %custom-call.20 = f32[2,128,128]{1,2,0:T(8,128)S(1)} custom-call(f32[2,128,128]{2,1,0:T(8,128)S(1)} %get-tuple-element.35), custom_call_target="InvertDiagBlocksLowerTriangular" | custom-call | tf_op jit(solution)/shard_map/triangular_solve/custom-call.0 | solution.py:29
  453.0 0.3 convolution_subtract_fusion.2
  453.6 0.7 fusion.8
  454.4 0.7 constant_dynamic-slice_fusion.2
  455.1 42.9 %all-gather.5.cloned.1.call-done = f32[4096,128]{0,1:T(8,128)} async-done(((f32[256,128]{0,1:T(8,128)}), f32[4096,128]{0,1:T(8,128)}) %all-gather.5.cloned.1.call-update) | async-done | bytes 2097168 | tf_op jit(solution)/shard_map/all_gather | solution.py:40
  498.0 4.0 reshape.45
  502.0 3.1 copy.33
  505.0 4.9 all-to-all-start.1
  510.0 1.0 pad_maximum_fusion
  511.0 1.0 copy.38
  512.0 0.9 fusion.28
  512.9 0.9 convolution_subtract_fusion.8
  514.1 1.8 fusion
  515.8 19.0 %all-to-all-done.1 = f32[8,2,256,128]{2,0,3,1:T(8,128)} async-done(((f32[8,2,256,128]{2,0,3,1:T(8,128)}), f32[8,2,256,128]{2,0,3,1:T(8,128)}, u32[]{:S(2)}, u32[]{:S(2)}) %all-to-all-start.1) | async-done | bytes 2097184 | tf_op jit(solution)/shard_map/all_to_all | solution.py:42
  534.8 2.5 copy.44
  537.2 4.9 convolution_subtract_fusion
  542.2 2.9 copy.37
  (68 shorter events, 4.6 us)
Async XLA Ops:
  7.2 27.6 %all-reduce.8.cloned.1.call-start = ((), (), s32[]{:S(2)}) async-start(), calls=%async_computation.2 | async-start | bytes 524288 | tf_op jit(solution)/shard_map/psum | solution.py:11
  7.2 2.8 copy-start.5
  9.2 143.2 %copy-start = (f32[256,2048]{0,1:T(8,128)}, f32[256,2048]{0,1:T(8,128)S(1)}, u32[]{:S(2)}) copy-start(f32[256,2048]{0,1:T(8,128)S(1)} %copy.27) | copy-start | bytes 6291460
  10.0 118.0 %all-reduce.14.cloned.1.call-start = ((), (), s32[]{:S(2)}) async-start(), calls=%async_computation.7 | async-start | bytes 655360 | tf_op jit(solution)/shard_map/psum | solution.py:11
  35.6 200.2 %all-gather.3.cloned.1.call-start = ((), (), s32[]{:S(2)}) async-start(), calls=%async_computation.3 | async-start | bytes 2228224 | tf_op jit(solution)/shard_map/all_gather | solution.py:40
  141.9 48.5 %copy-start.2 = (f32[256,256]{0,1:T(8,128)S(1)}, f32[256,256]{0,1:T(8,128)}, u32[]{:S(2)}) copy-start(f32[256,256]{0,1:T(8,128)} %all-reduce.8.cloned.1.call-done) | copy-start | bytes 786436
  240.3 4.0 copy-start.6
  240.3 28.6 %all-to-all-start = ((f32[8,2,256,128]{2,0,3,1:T(8,128)}), f32[8,2,256,128]{2,0,3,1:T(8,128)S(1)}, u32[]{:S(2)}, u32[]{:S(2)}) async-start(f32[8,2,256,128]{2,0,3,1:T(8,128)} %copy.26), calls=%async_computation | async-start | bytes 4194304 | tf_op jit(solution)/shard_map/all_to_all | solution.py:42
  244.2 52.3 %all-reduce.10.cloned.1.call-start = ((), (), s32[]{:S(2)}) async-start(), calls=%async_computation.4 | async-start | bytes 524288 | tf_op jit(solution)/shard_map/psum | solution.py:11
  268.9 1.6 copy-start.1
  274.9 114.7 %all-reduce.12.cloned.1.call-start = ((), (), s32[]{:S(2)}) async-start(), calls=%async_computation.6 | async-start | bytes 655360 | tf_op jit(solution)/shard_map/psum | solution.py:11
  297.3 200.7 %all-gather.5.cloned.1.call-start = ((), (), s32[]{:S(2)}) async-start(), calls=%async_computation.5 | async-start | bytes 2228224 | tf_op jit(solution)/shard_map/all_gather | solution.py:40
  403.5 49.1 %copy-start.3 = (f32[256,256]{0,1:T(8,128)S(1)}, f32[256,256]{0,1:T(8,128)}, u32[]{:S(2)}) copy-start(f32[256,256]{0,1:T(8,128)} %all-reduce.10.cloned.1.call-done) | copy-start | bytes 786436
  505.0 4.9 copy-start.4
  505.0 29.7 %all-to-all-start.1 = ((f32[8,2,256,128]{2,0,3,1:T(8,128)}), f32[8,2,256,128]{2,0,3,1:T(8,128)}, u32[]{:S(2)}, u32[]{:S(2)}) async-start(f32[8,2,256,128]{2,0,3,1:T(8,128)} %copy.33), calls=%async_computation.1 | async-start | bytes 4194304 | tf_op jit(solution)/shard_map/all_to_all | solution.py:42
Sparse Core Ops, SparseCore 0:
  10.8 23.9 all-reduce.7
  39.3 88.7 all-reduce.13
  193.0 42.7 all-gather.2
  275.1 21.4 all-reduce.9
  300.8 88.7 all-reduce.11
  455.2 42.7 all-gather.4
where the time goes:
time: 563 us; the launch traced here: 552 us
  waiting for transfers between devices  358 us (64%)
  other arithmetic  116 us (21%)
  local copies, waits for them, and re-layouts  33.8 us (6%)
  between operations  17.6 us (3%)
  matrix products  16.9 us (3%)
  starting transfers between devices  9.28 us (2%)
    psum x4, waiting for transfers between devices, broadcast(): return lax.psum(kept, axis)  229 us
    all_gather x2, waiting for transfers between devices, shards(): every = lax.all_gather(sliced, 'row', axis=0, tiled=True)  85.8 us
    another operation x13, other arithmetic, shards(): lower = jnp.linalg.cholesky(diagonal)  68.5 us
    all_to_all x2, waiting for transfers between devices, shards(): mine = lax.all_to_all(every, 'col', split_axis=1, concat_axis=3, tiled=True)  43.2 us
    another operation x5, other arithmetic, shards(): lax.linalg.triangular_solve(lower, column, left_side=False, lower=True, t...  39.4 us
    reshape x4, local copies, waits for them, and re-layouts, shards(): every = every.reshape(local_blocks, grid_cols, block, width)  11.6 us
  transfers between devices with their start and end apart: 8, of which 8 were waited for; matrix products, arithmetic and copies ran while one was open for 1% of the time, Pallas kernels for 0%

commit v1 on v0

v1 whole, which is shorter than its diff:
```python
import functools

import jax
import jax.numpy as jnp
from jax import lax
from jax.experimental import pallas as pl
from jax.experimental.pallas import tpu as pltpu
from jax.sharding import PartitionSpec as P

PANELS = 2
TILE = 128
F32 = jnp.float32
HIGHEST = lax.Precision.HIGHEST
NN = (((1,), (0,)), ((), ()))
NT = (((1,), (1,)), ((), ()))
TN = (((0,), (0,)), ((), ()))


def dot(a, b, dims):
    return lax.dot_general(a, b, dims, precision=HIGHEST, preferred_element_type=F32)


def split(a):
    high = a.astype(jnp.bfloat16)
    return high, (a - high.astype(F32)).astype(jnp.bfloat16)


def dot3(a, b, dims):
    (ah, al), (bh, bl) = a, b
    one = functools.partial(lax.dot_general, dimension_numbers=dims, preferred_element_type=F32)
    return one(ah, bh) + (one(ah, bl) + one(al, bh))


def eliminate(block):
    n = block.shape[0]
    lane = lax.broadcasted_iota(jnp.int32, (8, n), 1)
    sub = lax.broadcasted_iota(jnp.int32, (8, n), 0)
    tiles = [block[8 * t : 8 * t + 8] for t in range(n // 8)]

    def wide(x):
        return jnp.broadcast_to(x, (8, n))

    for p in range(0, n, 2):
        q, g, s = p + 1, p // 8, p % 8
        row_p = wide(tiles[g][s : s + 1])
        row_q = wide(tiles[g][s + 1 : s + 2])
        a, b, d = wide(row_p[:, p : p + 1]), wide(row_p[:, q : q + 1]), wide(row_q[:, q : q + 1])
        inv_a = 1.0 / a
        inv_q = a * (1.0 / (a * d - b * b))
        ratio = b * inv_a
        at_p, at_q = lane == p, lane == q
        pair = at_p | at_q
        new_q = jnp.where(at_p, -ratio, row_q - ratio * row_p)
        use_p = jnp.where(at_p, 1.0, jnp.where(at_q, 0.0, row_p))
        use_q = jnp.where(at_q, 1.0, new_q)
        for t in range(g, n // 8):
            col_p, col_q = wide(tiles[t][:, p : p + 1]), wide(tiles[t][:, q : q + 1])
            m_p = col_p * inv_a
            m_q = (col_q - m_p * b) * inv_q
            new = jnp.where(pair, 0.0, tiles[t]) - m_p * use_p - m_q * use_q
            if t == g:
                new = jnp.where(sub > s + 1, new, jnp.where(sub == s + 1, new_q, tiles[t]))
            tiles[t] = new
    return jnp.concatenate(tiles, axis=0)


def factorise(work):
    n = work.shape[0]
    rows = lax.broadcasted_iota(jnp.int32, (TILE, TILE), 0)
    cols = lax.broadcasted_iota(jnp.int32, (TILE, TILE), 1)
    row_id = lax.broadcasted_iota(jnp.int32, (n, n), 0)
    col_id = lax.broadcasted_iota(jnp.int32, (n, n), 1)
    lane = lax.broadcasted_iota(jnp.int32, (TILE, n), 1)

    def body(k, carry):
        at = pl.multiple_of(k * TILE, TILE)
        done = eliminate(work[pl.ds(at, TILE), pl.ds(at, TILE)])
        pivots = jnp.sum(jnp.where(rows == cols, done, 0.0), axis=1, keepdims=True)
        scale = 1.0 / jnp.sqrt(pivots)
        inverse = scale * jnp.where(rows > cols, done, jnp.where(rows == cols, 1.0, 0.0))
        work[pl.ds(at, TILE), :] = dot(inverse, work[pl.ds(at, TILE), :], NN)
        work[pl.ds(at, TILE), pl.ds(at, TILE)] = inverse
        strip = work[pl.ds(at, TILE), :]
        later = jnp.where(lane >= at + TILE, strip, 0.0)
        below = row_id >= at + TILE
        here = (col_id >= at) & (col_id < at + TILE)
        work[...] = jnp.where(below & here, 0.0, work[...]) - dot(later, strip, TN)
        return carry

    lax.fori_loop(0, n // TILE, body, 0)


def finish(my_row, my_col, work, own, head_rhs, matrix, rhs, gathered, out, factor, solved):
    block = matrix.shape[0]
    width = own.shape[1]
    row_id = lax.broadcasted_iota(jnp.int32, (width, width), 0)
    col_id = lax.broadcasted_iota(jnp.int32, (width, width), 1)
    inverse = jnp.where(row_id >= col_id, work[...], 0.0)
    rows = lax.broadcasted_iota(jnp.int32, (block, width), 0) + my_row * block
    cols = lax.broadcasted_iota(jnp.int32, (block, width), 1)
    panel = jnp.where(cols <= rows, dot(own[...], inverse, NT), 0.0)
    factor[...] = panel
    panel = jnp.where(cols < my_row * block, panel, 0.0)
    top = dot(inverse, head_rhs[...], NN)
    value = rhs[...] - dot(panel, top, NN)
    for k in range(width // block):
        value = jnp.where(my_row == k, top[k * block : (k + 1) * block], value)
    solved[...] = value
    weight = dot(panel, inverse, NN)
    first = jnp.where(my_col == 0, 0.0, weight)
    for k in range(1, width // block):
        part = dot(jnp.where(cols < k * block, panel, 0.0), inverse, NN)
        first = jnp.where(my_col == k, part, first)
    first, weight = split(first), split(weight)
    for m in range(matrix.shape[1] // block):
        here = slice(m * block, (m + 1) * block)
        other = split(gathered[m])
        out[:, here] = matrix[:, here] - dot3(first if m == 0 else weight, other, NT)


def local_kernel(head, own, head_rhs, matrix, rhs, gathered, out, factor, solved, work):
    work[...] = head[...]
    factorise(work)
    finish(
        lax.axis_index("row"), lax.axis_index("col"),
        work, own, head_rhs, matrix, rhs, gathered, out, factor, solved,
    )


def gather(matrix, targets):
    block = matrix.shape[0]
    mine = lax.axis_index("col")
    pieces = lax.all_gather(matrix[:, :block], "col", axis=0)
    own = jnp.concatenate([pieces[k] for k in range(PANELS)], axis=1)
    every = lax.all_gather(own, "row", axis=0)
    head = every[:PANELS].reshape(PANELS * block, PANELS * block)
    grid_cols = lax.axis_size("col")
    every = every.reshape(-1, grid_cols, block, PANELS * block)
    gathered = lax.dynamic_index_in_dim(every, mine, 1, keepdims=False)
    return head, own, gathered


def head_of(targets):
    my_row = lax.axis_index("row")
    kept = jnp.concatenate(
        [jnp.where(my_row == k, targets, F32(0.0)) for k in range(PANELS)], axis=0
    )
    return lax.psum(kept, "row")


def shards(matrix, targets):
    head_rhs = head_of(targets)
    head, own, gathered = gather(matrix, targets)
    block = matrix.shape[0]
    width = PANELS * block
    vmem = pl.BlockSpec(memory_space=pltpu.VMEM)
    return pl.pallas_call(
        local_kernel,
        out_shape=(
            jax.ShapeDtypeStruct(matrix.shape, F32),
            jax.ShapeDtypeStruct((block, width), F32),
            jax.ShapeDtypeStruct(targets.shape, F32),
        ),
        in_specs=[vmem] * 6,
        out_specs=(vmem, vmem, vmem),
        scratch_shapes=[pltpu.VMEM((width, width), F32)],
        compiler_params=pltpu.CompilerParams(vmem_limit_bytes=48 * 1024 * 1024),
    )(head, own, head_rhs, matrix, targets, gathered)


def solution(mesh):
    return jax.shard_map(
        shards,
        mesh=mesh,
        in_specs=(P("row", "col"), P("row", None)),
        out_specs=(P("row", "col"), P("row", None), P("row", None)),
        check_vma=False,
    )
```

time: 563 us -> 248 us (0.44); the launches traced: 552 us -> 246 us
  waiting for transfers between devices: 358 us -> 160 us
  other arithmetic: 116 us -> 1.6 us
  Pallas kernels: 0 us -> 51.1 us
  local copies, waits for them, and re-layouts: 33.8 us -> 11.1 us
  matrix products: 16.9 us -> 0 us
  starting transfers between devices: 9.28 us -> 0.08 us
  blocking collectives: 0 us -> 7.85 us
    psum x4 -> x1, waiting for transfers between devices: 229 us -> 85.4 us  [head_of(): return lax.psum(kept, 'row')]
    another operation x18 -> x0, other arithmetic: 108 us -> none  [the longest x13 68.5 us: shards(): lower = jnp.linalg.cholesky(diagonal)]
    pallas_call x0 -> x1, Pallas kernels: none -> 51.1 us  [shards(): pl.pallas_call(local_kernel, out_shape=(jax.ShapeDtypeStruct(matrix.shape...]
    all_to_all x2 -> x0, waiting for transfers between devices: 43.2 us -> none  [shards(): mine = lax.all_to_all(every, 'col', split_axis=1, concat_axis=3, tiled=True)]
    reshape x4 -> x0, local copies, waits for them, and re-layouts: 11.6 us -> none  [shards(): every = every.reshape(local_blocks, grid_cols, block, width)]
    dot_general x4 -> x0, matrix products: 11.3 us -> none  [the longest x2 8.61 us: shards(): matrix = matrix - jnp.dot(panel, partner.T, precision=lax.Precision.HIGHEST)]
    all_gather x2 -> x1, waiting for transfers between devices: 85.8 us -> 74.9 us  [gather(): every = lax.all_gather(own, 'row', axis=0)]
    another operation x33 -> x0, local copies, waits for them, and re-layouts: 8.83 us -> none  [the longest x23 8.39 us: shards(): lax.linalg.triangular_solve(lower, column, left_side=False, lower=True, t...]
  transfers between devices with their start and end apart: 8 -> 2, of which waited for: 8 -> 2; matrix products, arithmetic and copies ran while one was open for 1% -> 3% of each run, Pallas kernels for 0% -> 0%
where the time goes in v1:
time: 248 us; the launch traced here: 246 us
  waiting for transfers between devices  160 us (65%)
  Pallas kernels  51.1 us (21%)
  between operations  14.1 us (6%)
  local copies, waits for them, and re-layouts  11.1 us (4%)
  blocking collectives  7.85 us (3%)
    psum x1, waiting for transfers between devices, head_of(): return lax.psum(kept, 'row')  85.4 us
    all_gather x1, waiting for transfers between devices, gather(): every = lax.all_gather(own, 'row', axis=0)  74.9 us
    pallas_call x1, Pallas kernels, shards(): pl.pallas_call(local_kernel, out_shape=(jax.ShapeDtypeStruct(matrix.shape...  51.1 us
    all_gather x1, blocking collectives, gather(): pieces = lax.all_gather(matrix[:, :block], 'col', axis=0)  7.85 us
  transfers between devices with their start and end apart: 2, of which 2 were waited for; matrix products, arithmetic and copies ran while one was open for 3% of the time, Pallas kernels for 0%

profile of v1, /device:TPU:5, one launch (start us, length us, event | category | flops | bytes accessed | tf_op | source)
XLA Modules:
  0.0 246.1 jit_solution(6376391535375567976)
XLA Ops:
  7.2 0.0 all-gather.4.cloned.1.call-start
  7.2 1.0 slice.12
  8.2 7.9 %all-gather = f32[512,256]{1,0:T(8,128)S(1)} all-gather(f32[256,256]{1,0:T(8,128)S(1)} %slice.12), channel_id=2, replica_groups=mesh['row'=16,'col'=2] {'col'}, dimensions={0}, use_global_device_ids=true | all-gather | bytes 786432 | tf_op jit(solution)/shard_map/all_gather | solution.py:133
  16.1 0.9 pad_maximum_fusion.own
  16.9 0.0 all-gather.4.cloned.1.call-update
  17.0 0.0 all-reduce.2.cloned.1.call-start
  17.0 0.9 copy.5.rhs
  18.0 0.7 pad_maximum_fusion.1
  18.7 0.0 all-reduce.2.cloned.1.call-update
  18.7 74.9 %all-gather.4.cloned.1.call-done = f32[4096,512]{1,0:T(8,128)} async-done(((f32[256,512]{1,0:T(8,128)}), f32[4096,512]{1,0:T(8,128)}) %all-gather.4.cloned.1.call-update) | async-done | bytes 8388624 | tf_op jit(solution)/shard_map/all_gather | solution.py:135
  93.6 0.0 copy-start
  93.6 4.7 %dynamic-slice_bitcast_fusion.gathered = f32[8,256,512]{2,1,0:T(8,128)} fusion(f32[8,2,256,512]{3,2,1,0:T(8,128)} %bitcast.5, s32[]{:T(128)S(6)} %select_n.22), kind=kLoop, calls=%fused_computation | loop fusion | bytes 8388612 | tf_op jit(solution)/shard_map/jit(dynamic_index_in_dim)/squeeze | solution.py:139
  98.2 1.3 slice.21.head
  99.5 85.4 %all-reduce.2.cloned.1.call-done.head_rhs = f32[512,64]{1,0:T(8,128)} async-done(((f32[512,64]{1,0:T(8,128)}), f32[512,64]{1,0:T(8,128)}) %all-reduce.2.cloned.1.call-update) | async-done | bytes 131088 | tf_op jit(solution)/shard_map/psum | solution.py:148
  184.9 0.0 copy-done
  184.9 0.0 copy-start.1
  184.9 1.6 copy-done.1
  186.5 0.0 copy-start.2
  186.5 0.9 copy-done.2
  187.5 51.1 %shard_map.49 = (f32[256,2048]{1,0:T(8,128)}, f32[256,512]{1,0:T(8,128)}, f32[256,64]{1,0:T(8,128)S(1)}) custom-call(f32[512,512]{1,0:T(8,128)S(1)} %slice.21.head, f32[256,512]{1,0:T(8,128)S(1)} %copy-done, f32[512,64]{1,0:T(8,128)S(1)} %copy-done.2, f32[256,2048]{1,0:T(8,128)S(1)} %copy-done.1, f32[256,64]{1,0:T(8,128)S(1)} %copy.5.rhs, ...), custom_call_target="tpu_custom_call" | custom-call | tf_op jit(solution)/shard_map/pallas_call | solution.py:157
  238.6 0.7 copy.9
  (2 shorter events, 0.1 us)
Async XLA Ops:
  7.2 86.4 %all-gather.4.cloned.1.call-start = ((), (), s32[]{:S(2)}) async-start(), calls=%async_computation.1 | async-start | bytes 8912896 | tf_op jit(solution)/shard_map/all_gather | solution.py:135
  17.0 168.0 %all-reduce.2.cloned.1.call-start = ((), (), s32[]{:S(2)}) async-start(), calls=%async_computation | async-start | bytes 524288 | tf_op jit(solution)/shard_map/psum | solution.py:148
  93.6 91.3 %copy-start = (f32[256,512]{1,0:T(8,128)S(1)}, f32[256,512]{1,0:T(8,128)}, u32[]{:S(2)}) copy-start(f32[256,512]{1,0:T(8,128)} %pad_maximum_fusion.own) | copy-start | bytes 1572868
  184.9 1.6 copy-start.1
  186.5 0.9 copy-start.2
Sparse Core Ops, SparseCore 0:
  17.1 76.4 all-gather.3
  97.5 87.3 all-reduce.1

commit v2 on v1

--- a/solution.py
+++ b/solution.py
@@ -64,7 +64,7 @@
     return jnp.concatenate(tiles, axis=0)
 
 
-def factorise(work):
+def factorise(work, between):
     n = work.shape[0]
     rows = lax.broadcasted_iota(jnp.int32, (TILE, TILE), 0)
     cols = lax.broadcasted_iota(jnp.int32, (TILE, TILE), 1)
@@ -72,8 +72,8 @@
     col_id = lax.broadcasted_iota(jnp.int32, (n, n), 1)
     lane = lax.broadcasted_iota(jnp.int32, (TILE, n), 1)
 
-    def body(k, carry):
-        at = pl.multiple_of(k * TILE, TILE)
+    for k in range(n // TILE):
+        at = k * TILE
         done = eliminate(work[pl.ds(at, TILE), pl.ds(at, TILE)])
         pivots = jnp.sum(jnp.where(rows == cols, done, 0.0), axis=1, keepdims=True)
         scale = 1.0 / jnp.sqrt(pivots)
@@ -85,12 +85,10 @@
         below = row_id >= at + TILE
         here = (col_id >= at) & (col_id < at + TILE)
         work[...] = jnp.where(below & here, 0.0, work[...]) - dot(later, strip, TN)
-        return carry
-
-    lax.fori_loop(0, n // TILE, body, 0)
-
-
-def finish(my_row, my_col, work, own, head_rhs, matrix, rhs, gathered, out, factor, solved):
+        between(k)
+
+
+def finish(my_row, my_col, work, own, head, head_rhs, matrix, rhs, gathered, out, factor, solved):
     block = matrix.shape[0]
     width = own.shape[1]
     row_id = lax.broadcasted_iota(jnp.int32, (width, width), 0)
@@ -114,17 +112,257 @@
     first, weight = split(first), split(weight)
     for m in range(matrix.shape[1] // block):
         here = slice(m * block, (m + 1) * block)
-        other = split(gathered[m])
+        other = gathered[m]
+        if m == 0 and head is not None:
+            other = head[pl.ds(pl.multiple_of(my_col * block, block), block), :]
+        other = split(other)
         out[:, here] = matrix[:, here] - dot3(first if m == 0 else weight, other, NT)
 
 
 def local_kernel(head, own, head_rhs, matrix, rhs, gathered, out, factor, solved, work):
     work[...] = head[...]
-    factorise(work)
+    factorise(work, lambda k: None)
     finish(
         lax.axis_index("row"), lax.axis_index("col"),
-        work, own, head_rhs, matrix, rhs, gathered, out, factor, solved,
+        work, own, None, head_rhs, matrix, rhs, gathered, out, factor, solved,
     )
+
+
+CHUNKS = 4
+MESH = pl.DeviceIdType.MESH
+
+
+def fused_kernel(
+    matrix, rhs, out, factor, solved, work, own, head, head_rhs, gathered,
+    head_send, head_recv, ring_send, ring_recv, core_send, core_recv, swap_send, swap_recv,
+):
+    block = matrix.shape[0]
+    half, chunk = block // 2, block // CHUNKS
+    my_row, col = lax.axis_index("row"), lax.axis_index("col")
+    chips = lax.axis_size("row") // 2
+    far = chips // 2
+    chip, core = my_row // 2, lax.rem(my_row, 2)
+
+    def chip_at(place):
+        return jnp.where(place < far, 2 * place, 2 * (chips - 1 - place) + 1)
+
+    place = jnp.where(lax.rem(chip, 2) == 0, chip // 2, chips - 1 - chip // 2)
+    right = (2 * chip_at(lax.rem(place + 1, chips)) + core, col)
+    left = (2 * chip_at(lax.rem(place + chips - 1, chips)) + core, col)
+    sibling = (2 * chip + 1 - core, col)
+    across = (my_row, 1 - col)
+    cross = (2 * chip + 1 - core, 1 - col)
+
+    def copy(src, dst, send, recv, device):
+        return pltpu.make_async_remote_copy(
+            src_ref=src, dst_ref=dst, send_sem=send, recv_sem=recv,
+            device_id=device, device_id_type=MESH,
+        )
+
+    def when(condition, action):
+        pl.when(condition)(action)
+
+    def panel_at(index):
+        return pl.ds(pl.multiple_of(index * block, block), block)
+
+    def rows_at(index, size):
+        return pl.ds(pl.multiple_of(index * size, size), size)
+
+    barrier = pltpu.get_barrier_semaphore()
+    for device in (right, left, sibling, across, cross):
+        pl.semaphore_signal(barrier, inc=1, device_id=device, device_id_type=MESH)
+    pl.semaphore_wait(barrier, 5)
+
+    def head_part(i, on_core, on_col):
+        if i == CHUNKS:
+            return head_rhs.at[panel_at(on_core), :]
+        return head.at[
+            pl.ds(pl.multiple_of(on_core * block + i * chunk, chunk), chunk), panel_at(on_col)
+        ]
+
+    def head_copy(kind, i, device, on_core, on_col):
+        part = head_part(i, on_core, on_col)
+        return copy(part, part, head_send.at[kind, i], head_recv.at[kind, i], device)
+
+    def head_right(i):
+        part = head_part(i, core, col)
+        return copy(part, part, head_send.at[0, i], head_recv.at[0, i], right)
+
+    def head_left(i):
+        part = head_part(i, core, col)
+        return copy(part, part, head_send.at[1, i], head_recv.at[0, i], left)
+
+    sends_right = place < far
+    sends_left = (place == 0) | (place > far + 1)
+
+    @pl.when(place == 0)
+    def _():
+        head[panel_at(core), panel_at(col)] = matrix[:, :block]
+        head_rhs[panel_at(core), :] = rhs[...]
+
+    own[:, panel_at(col)] = matrix[:, :block]
+    mine = core == col
+
+    def swap_same():
+        here = rows_at(1 - core, half)
+        return copy(
+            matrix.at[here, pl.ds(0, block)],
+            gathered.at[chip, here, panel_at(col)],
+            swap_send.at[0], swap_recv.at[0], sibling,
+        )
+
+    def swap_over(kind, to_core, device):
+        here = rows_at(to_core, half)
+        return copy(
+            matrix.at[here, pl.ds(0, block)],
+            gathered.at[chip, here, panel_at(col)],
+            swap_send.at[kind], swap_recv.at[1], device,
+        )
+
+    own_copy = copy(
+        matrix.at[:, pl.ds(0, block)], own.at[:, panel_at(col)], swap_send.at[3], swap_recv.at[3], across
+    )
+
+    for i in range(CHUNKS + 1):
+        when(place > 0, lambda i=i: head_right(i).wait_recv())
+        when(sends_right, lambda i=i: head_right(i).start())
+        when(sends_left, lambda i=i: head_left(i).start())
+        if i < CHUNKS:
+            head_copy(2, i, across, core, col).start()
+        head_copy(3, i, sibling, core, col).start()
+
+    @pl.when(mine)
+    def _():
+        here = rows_at(core, half)
+        gathered[chip, here, panel_at(col)] = matrix[here, :block]
+        swap_same().start()
+
+    @pl.when(jnp.logical_not(mine))
+    def _():
+        swap_over(1, core, across).start()
+        swap_over(2, 1 - core, cross).start()
+
+    for i in range(CHUNKS):
+        part = head_part(i, core, 1 - col)
+        copy(part, part, head_send.at[2, i], head_recv.at[2, i], across).wait_recv()
+        head_copy(4, i, sibling, core, 1 - col).start()
+    own_copy.start()
+    for i in range(CHUNKS):
+        for kind, on_col in ((3, col), (4, 1 - col)):
+            part = head_part(i, 1 - core, on_col)
+            copy(part, part, head_send.at[kind, i], head_recv.at[kind, i], sibling).wait_recv()
+    work[...] = head[...]
+
+    def piece(origin, on_core, part=None):
+        start, size = on_core * half, half
+        if part is not None:
+            start, size = start + part * (half // 2), half // 2
+        return gathered.at[chip_at(origin), pl.ds(pl.multiple_of(start, size), size), :]
+
+    def origin(direction, step):
+        return lax.rem(place + (chips - step if direction == 0 else step), chips)
+
+    def ring_copy(direction, step, source):
+        part = direction if step == far else None
+        ref = piece(source, core, part)
+        return copy(
+            ref, ref, ring_send.at[direction, step], ring_recv.at[direction, step],
+            left if direction else right,
+        )
+
+    def core_copy(index, source, on_core):
+        ref = piece(source, on_core)
+        return copy(ref, ref, core_send.at[index], core_recv.at[index], sibling)
+
+    def ring_start(step):
+        for direction in range(2):
+            source = origin(direction, step - 1)
+            when(source > 0, lambda d=direction, o=source: ring_copy(d, step, o).start())
+
+    arrivals = [(0, place)] + [
+        (1 + direction * (far - 1) + step - 1, origin(direction, step))
+        for direction in range(2) for step in range(1, far)
+    ] + [(2 * far - 1, origin(0, far))]
+
+    def ring_step(step):
+        for direction in range(2):
+            source = origin(direction, step)
+            when(source > 0, lambda d=direction, o=source: ring_copy(d, step, o).wait_recv())
+        if step < far:
+            ring_start(step + 1)
+            for direction in range(2):
+                source = origin(direction, step)
+                index = 1 + direction * (far - 1) + step - 1
+                when(source > 0, lambda n=index, o=source: core_copy(n, o, core).start())
+        else:
+            source = origin(0, far)
+            when(source > 0, lambda: core_copy(2 * far - 1, source, core).start())
+
+    when(jnp.logical_not(mine), lambda: swap_same().wait_recv())
+    swap_over(1, core, across).wait_recv()
+    ring_start(1)
+    when(place > 0, lambda: core_copy(0, place, core).start())
+
+    steps = work.shape[0] // TILE
+    factorise(work, lambda k: [ring_step(s) for s in range(1, far + 1) if min(s, steps) == k + 1])
+
+    for index, source in arrivals:
+        when(source > 0, lambda n=index, o=source: core_copy(n, o, 1 - core).wait_recv())
+    own_copy.wait_recv()
+    part = head_part(CHUNKS, 1 - core, col)
+    copy(part, part, head_send.at[3, CHUNKS], head_recv.at[3, CHUNKS], sibling).wait_recv()
+
+    finish(my_row, col, work, own, head, head_rhs, matrix, rhs, gathered, out, factor, solved)
+
+    for i in range(CHUNKS + 1):
+        when(sends_right, lambda i=i: head_right(i).wait_send())
+        when(sends_left, lambda i=i: head_left(i).wait_send())
+        head_copy(3, i, sibling, core, col).wait_send()
+        if i < CHUNKS:
+            head_copy(2, i, across, core, col).wait_send()
+            head_copy(4, i, sibling, core, 1 - col).wait_send()
+    when(mine, lambda: swap_same().wait_send())
+    for kind, to_core, device in ((1, core, across), (2, 1 - core, cross)):
+        when(jnp.logical_not(mine), lambda k=kind, t=to_core, d=device: swap_over(k, t, d).wait_send())
+    own_copy.wait_send()
+    for step in range(1, far + 1):
+        for direction in range(2):
+            source = origin(direction, step - 1)
+            when(source > 0, lambda d=direction, s=step, o=source: ring_copy(d, s, o).wait_send())
+    for index, source in arrivals:
+        when(source > 0, lambda n=index, o=source: core_copy(n, o, core).wait_send())
+
+
+def fused(matrix, targets):
+    block = matrix.shape[0]
+    width = PANELS * block
+    chips = lax.axis_size("row") // 2
+    vmem = pl.BlockSpec(memory_space=pltpu.VMEM)
+    dma = pltpu.SemaphoreType.DMA
+    return pl.pallas_call(
+        fused_kernel,
+        out_shape=(
+            jax.ShapeDtypeStruct(matrix.shape, F32),
+            jax.ShapeDtypeStruct((block, width), F32),
+            jax.ShapeDtypeStruct(targets.shape, F32),
+        ),
+        in_specs=[vmem] * 2,
+        out_specs=(vmem, vmem, vmem),
+        scratch_shapes=[
+            pltpu.VMEM((width, width), F32),
+            pltpu.VMEM((block, width), F32),
+            pltpu.VMEM((width, width), F32),
+            pltpu.VMEM((width, targets.shape[1]), F32),
+            pltpu.VMEM((chips, block, width), F32),
+            dma((5, CHUNKS + 1)), dma((5, CHUNKS + 1)),
+            dma((2, chips // 2 + 1)), dma((2, chips // 2 + 1)),
+            dma((chips,)), dma((chips,)),
+            dma((4,)), dma((4,)),
+        ],
+        compiler_params=pltpu.CompilerParams(
+            vmem_limit_bytes=48 * 1024 * 1024, collective_id=0, has_side_effects=True
+        ),
+    )(matrix, targets)
 
 
 def gather(matrix, targets):
@@ -149,6 +387,9 @@
 
 
 def shards(matrix, targets):
+    rows = lax.axis_size("row")
+    if lax.axis_size("col") == PANELS == 2 and rows % 4 == 0 and rows >= 8:
+        return fused(matrix, targets)
     head_rhs = head_of(targets)
     head, own, gathered = gather(matrix, targets)
     block = matrix.shape[0]

time: 248 us -> 83 us (0.33)
  the two profiles are of different devices: /device:TPU:5 before, /device:TPU:29 now
where the time goes in v2:
time: 83 us; the launch traced here: 82.8 us
  Pallas kernels  76.8 us (93%)
  local copies, waits for them, and re-layouts  5.34 us (6%)
    pallas_call x1, Pallas kernels, fused(): pl.pallas_call(fused_kernel, out_shape=(jax.ShapeDtypeStruct(matrix.shape...  76.8 us
    unnamed x5, local copies, waits for them, and re-layouts  4.63 us

profile of v2, /device:TPU:29, one launch (start us, length us, event | category | flops | bytes accessed | tf_op | source)
XLA Modules:
  0.0 82.8 jit_solution(7263837371666951005)
XLA Ops:
  0.6 0.9 %copy.5.rhs = f32[256,64]{1,0:T(8,128)S(1)} copy(f32[256,64]{0,1:T(8,128)} %param.3) | data formatting | bytes 131072 | tf_op args[1]
  1.6 0.0 copy-start
  1.6 1.6 %copy-done = f32[256,2048]{1,0:T(8,128)S(1)} copy-done((f32[256,2048]{1,0:T(8,128)S(1)}, f32[256,2048]{1,0:T(8,128)}, u32[]{:S(2)}) %copy-start) | copy-done | bytes 2097176
  3.2 76.8 %shard_map.49 = (f32[256,2048]{1,0:T(8,128)S(1)}, f32[256,512]{1,0:T(8,128)S(1)}, f32[256,64]{1,0:T(8,128)S(1)}) custom-call(f32[256,2048]{1,0:T(8,128)S(1)} %copy-done, f32[256,64]{1,0:T(8,128)S(1)} %copy.5.rhs), custom_call_target="tpu_custom_call" | custom-call | tf_op jit(solution)/shard_map/pallas_call | solution.py:342
  79.9 0.7 copy.6
  80.7 1.3 %copy.9 = f32[256,2048]{1,0:T(8,128)} copy(f32[256,2048]{1,0:T(8,128)S(1)} %get-tuple-element.9) | data formatting | bytes 4194304
  82.0 0.8 copy.10
Async XLA Ops:
  1.6 1.6 %copy-start = (f32[256,2048]{1,0:T(8,128)S(1)}, f32[256,2048]{1,0:T(8,128)}, u32[]{:S(2)}) copy-start(f32[256,2048]{1,0:T(8,128)} %matrix.1) | copy-start | bytes 6291460

commit v3 on v2

--- a/solution.py
+++ b/solution.py
@@ -40,26 +40,45 @@
     def wide(x):
         return jnp.broadcast_to(x, (8, n))
 
-    for p in range(0, n, 2):
-        q, g, s = p + 1, p // 8, p % 8
-        row_p = wide(tiles[g][s : s + 1])
-        row_q = wide(tiles[g][s + 1 : s + 2])
-        a, b, d = wide(row_p[:, p : p + 1]), wide(row_p[:, q : q + 1]), wide(row_q[:, q : q + 1])
-        inv_a = 1.0 / a
-        inv_q = a * (1.0 / (a * d - b * b))
-        ratio = b * inv_a
-        at_p, at_q = lane == p, lane == q
-        pair = at_p | at_q
-        new_q = jnp.where(at_p, -ratio, row_q - ratio * row_p)
-        use_p = jnp.where(at_p, 1.0, jnp.where(at_q, 0.0, row_p))
-        use_q = jnp.where(at_q, 1.0, new_q)
+    for p in range(0, n, 4):
+        g, s = p // 8, p % 8
+        quad = (lane >= p) & (lane < p + 4)
+        kept = jnp.where(quad, 0.0, tiles[g])
+        columns = [wide(tiles[g][:, p + i : p + i + 1]) for i in range(4)]
+        a00, a10, a20, a30 = (wide(columns[0][s + i : s + i + 1]) for i in range(4))
+        a11, a21, a31 = (wide(columns[1][s + i : s + i + 1]) for i in range(1, 4))
+        a22, a32 = (wide(columns[2][s + i : s + i + 1]) for i in range(2, 4))
+        a33 = wide(columns[3][s + 3 : s + 4])
+        inv0 = 1.0 / a00
+        inv1 = a00 * (1.0 / (a00 * a11 - a10 * a10))
+        l10, l20, l30 = a10 * inv0, a20 * inv0, a30 * inv0
+        c21, c31 = a21 - a20 * l10, a31 - a30 * l10
+        l21, l31 = c21 * inv1, c31 * inv1
+        s22 = a22 - l20 * a20 - l21 * c21
+        s32 = a32 - l30 * a20 - l31 * c21
+        s33 = a33 - l30 * a30 - l31 * c31
+        inv2 = 1.0 / s22
+        inv3 = s22 * (1.0 / (s22 * s33 - s32 * s32))
+        l32 = s32 * inv2
+        unit = [jnp.where(lane == p + i, 1.0, wide(kept[s + i : s + i + 1])) for i in range(4)]
+        u0 = unit[0]
+        u1 = unit[1] - l10 * u0
+        u2 = unit[2] - l20 * u0 - l21 * u1
+        u3 = unit[3] - l30 * u0 - l31 * u1 - l32 * u2
         for t in range(g, n // 8):
-            col_p, col_q = wide(tiles[t][:, p : p + 1]), wide(tiles[t][:, q : q + 1])
-            m_p = col_p * inv_a
-            m_q = (col_q - m_p * b) * inv_q
-            new = jnp.where(pair, 0.0, tiles[t]) - m_p * use_p - m_q * use_q
             if t == g:
-                new = jnp.where(sub > s + 1, new, jnp.where(sub == s + 1, new_q, tiles[t]))
+                c0, c1, c2, c3 = columns
+            else:
+                c0, c1, c2, c3 = (wide(tiles[t][:, p + i : p + i + 1]) for i in range(4))
+            c1 = c1 - c0 * l10
+            c2 = c2 - c0 * l20 - c1 * l21
+            c3 = c3 - c0 * l30 - c1 * l31 - c2 * l32
+            base = kept if t == g else jnp.where(quad, 0.0, tiles[t])
+            new = base - (c0 * inv0) * u0 - (c1 * inv1) * u1 - (c2 * inv2) * u2 - (c3 * inv3) * u3
+            if t == g:
+                new = jnp.where(sub > s + 3, new, tiles[g])
+                for i, (u, inv) in enumerate(((u0, inv0), (u1, inv1), (u2, inv2), (u3, inv3))):
+                    new = jnp.where(sub == s + i, u * jnp.sqrt(inv), new)
             tiles[t] = new
     return jnp.concatenate(tiles, axis=0)
 
@@ -68,24 +87,27 @@
     n = work.shape[0]
     rows = lax.broadcasted_iota(jnp.int32, (TILE, TILE), 0)
     cols = lax.broadcasted_iota(jnp.int32, (TILE, TILE), 1)
-    row_id = lax.broadcasted_iota(jnp.int32, (n, n), 0)
-    col_id = lax.broadcasted_iota(jnp.int32, (n, n), 1)
-    lane = lax.broadcasted_iota(jnp.int32, (TILE, n), 1)
-
-    for k in range(n // TILE):
-        at = k * TILE
-        done = eliminate(work[pl.ds(at, TILE), pl.ds(at, TILE)])
-        pivots = jnp.sum(jnp.where(rows == cols, done, 0.0), axis=1, keepdims=True)
-        scale = 1.0 / jnp.sqrt(pivots)
-        inverse = scale * jnp.where(rows > cols, done, jnp.where(rows == cols, 1.0, 0.0))
-        work[pl.ds(at, TILE), :] = dot(inverse, work[pl.ds(at, TILE), :], NN)
-        work[pl.ds(at, TILE), pl.ds(at, TILE)] = inverse
-        strip = work[pl.ds(at, TILE), :]
-        later = jnp.where(lane >= at + TILE, strip, 0.0)
-        below = row_id >= at + TILE
-        here = (col_id >= at) & (col_id < at + TILE)
-        work[...] = jnp.where(below & here, 0.0, work[...]) - dot(later, strip, TN)
-        between(k)
+    diagonal = work[:TILE, :TILE]
+    for at in range(0, n, TILE):
+        end = at + TILE
+        inverse = jnp.where(rows >= cols, eliminate(diagonal), 0.0)
+        if end == n:
+            if at > 0:
+                work[at:end, :at] = dot(inverse, work[at:end, :at], NN)
+            work[at:end, at:end] = inverse
+            between(at // TILE)
+            return
+        after = dot(inverse, work[at:end, end:], NN)
+        nearest = after[:, :TILE]
+        diagonal = work[end : end + TILE, end : end + TILE] - dot(nearest, nearest, TN)
+        between(at // TILE)
+        work[end:, end:] = work[end:, end:] - dot(after, after, TN)
+        work[end:, at:end] = -dot(after, inverse, TN)
+        if at > 0:
+            before = dot(inverse, work[at:end, :at], NN)
+            work[at:end, :at] = before
+            work[end:, :at] = work[end:, :at] - dot(after, before, TN)
+        work[at:end, at:end] = inverse
 
 
 def finish(my_row, my_col, work, own, head, head_rhs, matrix, rhs, gathered, out, factor, solved):

time: 83 us -> 83.2 us (level)
  the two profiles are of different devices: /device:TPU:29 before, /device:TPU:5 now
where the time goes in v3:
time: 83.2 us; the launch traced here: 83 us
  Pallas kernels  77 us (93%)
  local copies, waits for them, and re-layouts  5.34 us (6%)
    pallas_call x1, Pallas kernels, fused(): pl.pallas_call(fused_kernel, out_shape=(jax.ShapeDtypeStruct(matrix.shape...  77 us
    unnamed x5, local copies, waits for them, and re-layouts  4.63 us

profile of v3, /device:TPU:5, one launch (start us, length us, event | category | flops | bytes accessed | tf_op | source)
XLA Modules:
  0.0 83.0 jit_solution(11699786231319959092)
XLA Ops:
  0.6 0.9 %copy.5.rhs = f32[256,64]{1,0:T(8,128)S(1)} copy(f32[256,64]{0,1:T(8,128)} %param.3) | data formatting | bytes 131072 | tf_op args[1]
  1.6 0.0 copy-start
  1.6 1.6 %copy-done = f32[256,2048]{1,0:T(8,128)S(1)} copy-done((f32[256,2048]{1,0:T(8,128)S(1)}, f32[256,2048]{1,0:T(8,128)}, u32[]{:S(2)}) %copy-start) | copy-done | bytes 2097176
  3.2 77.0 %shard_map.49 = (f32[256,2048]{1,0:T(8,128)S(1)}, f32[256,512]{1,0:T(8,128)S(1)}, f32[256,64]{1,0:T(8,128)S(1)}) custom-call(f32[256,2048]{1,0:T(8,128)S(1)} %copy-done, f32[256,64]{1,0:T(8,128)S(1)} %copy.5.rhs), custom_call_target="tpu_custom_call" | custom-call | tf_op jit(solution)/shard_map/pallas_call | solution.py:364
  80.2 0.7 copy.6
  80.9 1.3 %copy.9 = f32[256,2048]{1,0:T(8,128)} copy(f32[256,2048]{1,0:T(8,128)S(1)} %get-tuple-element.9) | data formatting | bytes 4194304
  82.2 0.8 copy.10
Async XLA Ops:
  1.6 1.6 %copy-start = (f32[256,2048]{1,0:T(8,128)S(1)}, f32[256,2048]{1,0:T(8,128)}, u32[]{:S(2)}) copy-start(f32[256,2048]{1,0:T(8,128)} %matrix.1) | copy-start | bytes 6291460

commit v4 on v3

--- a/solution.py
+++ b/solution.py
@@ -9,6 +9,7 @@
 
 PANELS = 2
 TILE = 128
+STRIP = 32
 F32 = jnp.float32
 HIGHEST = lax.Precision.HIGHEST
 NN = (((1,), (0,)), ((), ()))
@@ -33,15 +34,34 @@
 
 def eliminate(block):
     n = block.shape[0]
+    lane = lax.broadcasted_iota(jnp.int32, (STRIP, n), 1)
+    row = lax.broadcasted_iota(jnp.int32, (STRIP, n), 0)
+    strips = []
+    below = block
+    for at in range(0, n, STRIP):
+        strip = eliminate_strip(below[:STRIP], at)
+        strips.append(strip)
+        if at + STRIP < n:
+            inside = (lane >= at) & (lane < at + STRIP)
+            right = jnp.where(inside & (lane > at + row), 0.0, strip)
+            rest = n - at - STRIP
+            wide_lane = lax.broadcasted_iota(jnp.int32, (rest, n), 1)
+            cleared = jnp.where((wide_lane >= at) & (wide_lane < at + STRIP), 0.0, below[STRIP:])
+            below = cleared - dot(strip, right, TN)[at + STRIP :]
+    return jnp.concatenate(strips, axis=0)
+
+
+def eliminate_strip(strip, at):
+    n = strip.shape[1]
     lane = lax.broadcasted_iota(jnp.int32, (8, n), 1)
     sub = lax.broadcasted_iota(jnp.int32, (8, n), 0)
-    tiles = [block[8 * t : 8 * t + 8] for t in range(n // 8)]
+    tiles = [strip[8 * t : 8 * t + 8] for t in range(STRIP // 8)]
 
     def wide(x):
         return jnp.broadcast_to(x, (8, n))
 
-    for p in range(0, n, 4):
-        g, s = p // 8, p % 8
+    for p in range(at, at + STRIP, 4):
+        g, s = (p - at) // 8, p % 8
         quad = (lane >= p) & (lane < p + 4)
         kept = jnp.where(quad, 0.0, tiles[g])
         columns = [wide(tiles[g][:, p + i : p + i + 1]) for i in range(4)]
@@ -65,7 +85,7 @@
         u1 = unit[1] - l10 * u0
         u2 = unit[2] - l20 * u0 - l21 * u1
         u3 = unit[3] - l30 * u0 - l31 * u1 - l32 * u2
-        for t in range(g, n // 8):
+        for t in range(g, STRIP // 8):
             if t == g:
                 c0, c1, c2, c3 = columns
             else:

time: 83.2 us -> 75.3 us (0.905)
  Pallas kernels: 77 us -> 69.1 us
    pallas_call x1, Pallas kernels: 77 us -> 69.1 us  [fused(): pl.pallas_call(fused_kernel, out_shape=(jax.ShapeDtypeStruct(matrix.shape...]
where the time goes in v4:
time: 75.3 us; the launch traced here: 75.1 us
  Pallas kernels  69.1 us (92%)
  local copies, waits for them, and re-layouts  5.34 us (7%)
    pallas_call x1, Pallas kernels, fused(): pl.pallas_call(fused_kernel, out_shape=(jax.ShapeDtypeStruct(matrix.shape...  69.1 us
    unnamed x5, local copies, waits for them, and re-layouts  4.63 us

profile of v4, /device:TPU:5, one launch (start us, length us, event | category | flops | bytes accessed | tf_op | source)
XLA Modules:
  0.0 75.1 jit_solution(1804180626195175623)
XLA Ops:
  0.6 0.9 %copy.5.rhs = f32[256,64]{1,0:T(8,128)S(1)} copy(f32[256,64]{0,1:T(8,128)} %param.3) | data formatting | bytes 131072 | tf_op args[1]
  1.6 0.0 copy-start
  1.6 1.6 %copy-done = f32[256,2048]{1,0:T(8,128)S(1)} copy-done((f32[256,2048]{1,0:T(8,128)S(1)}, f32[256,2048]{1,0:T(8,128)}, u32[]{:S(2)}) %copy-start) | copy-done | bytes 2097176
  3.2 69.1 %shard_map.49 = (f32[256,2048]{1,0:T(8,128)S(1)}, f32[256,512]{1,0:T(8,128)S(1)}, f32[256,64]{1,0:T(8,128)S(1)}) custom-call(f32[256,2048]{1,0:T(8,128)S(1)} %copy-done, f32[256,64]{1,0:T(8,128)S(1)} %copy.5.rhs), custom_call_target="tpu_custom_call" | custom-call | tf_op jit(solution)/shard_map/pallas_call | solution.py:384
  72.3 0.7 copy.6
  73.0 1.3 %copy.9 = f32[256,2048]{1,0:T(8,128)} copy(f32[256,2048]{1,0:T(8,128)S(1)} %get-tuple-element.9) | data formatting | bytes 4194304
  74.3 0.8 %copy.10 = f32[256,512]{1,0:T(8,128)} copy(f32[256,512]{1,0:T(8,128)S(1)} %get-tuple-element.10) | data formatting | bytes 1048576
Async XLA Ops:
  1.6 1.6 %copy-start = (f32[256,2048]{1,0:T(8,128)S(1)}, f32[256,2048]{1,0:T(8,128)}, u32[]{:S(2)}) copy-start(f32[256,2048]{1,0:T(8,128)} %matrix.1) | copy-start | bytes 6291460
